TPU v7x, 256 devices: a whole 4x4x8 slice. The times are simulated.
256 devices in a mesh: pipe: 64 (over y, x, z_hi, core), tp: 4 (over z_lo).
Axes of the slice: x: 4, y: 4, z: 8 (z_hi: 2, z_lo: 4; z = z_hi * 4 + z_lo), core: 2. Of those that a mesh axis runs over, the one named last changes fastest.
Arguments:
- checkpoint: bfloat16 [64, 3, 512, 6144], P('pipe', None, 'tp'), may hold values from -6 to 6
- grad_out: bfloat16 [64, 512, 6144], P('pipe', 'tp'), may hold values from -6 to 6
Outputs:
- qkv_grad: bfloat16 [64, 3, 512, 6144], P('pipe', None, 'tp')
All inputs are finite; a program needn't handle non-finite values.
Results may differ from a plain program's by a relative error of at most 0.0087.
Values may be sent and summed in bfloat16 or wider, within the bound.
A program may use at most 128 MiB of HBM per device.

v0:
```python
import functools

import jax
import jax.numpy as jnp
from jax import lax
from jax.experimental import pallas as pl
from jax.experimental.pallas import tpu as pltpu
from jax.sharding import PartitionSpec as P

HEAD_DIM = 128
MESH = pl.DeviceIdType.MESH
AHEAD = 3
NT = (((1,), (1,)), ((), ()))
NN = (((1,), (0,)), ((), ()))
TN = (((0,), (0,)), ((), ()))


def dot(a, b, dims):
    return lax.dot_general(a, b, dims, preferred_element_type=jnp.float32)


def head_back(q, k, v, g):
    length = q.shape[0]
    scale = HEAD_DIM ** (-0.5)
    scores = dot(q, k, NT) * scale
    rows = lax.broadcasted_iota(jnp.int32, (length, length), 0)
    cols = lax.broadcasted_iota(jnp.int32, (length, length), 1)
    scores = jnp.where(cols <= rows, scores, jnp.float32(-1e30))
    top = jnp.max(scores, axis=-1, keepdims=True)
    expd = jnp.exp(scores - top)
    probs = expd / jnp.sum(expd, axis=-1, keepdims=True)
    probs_b = probs.astype(jnp.bfloat16)
    dprobs = dot(g, v, NT)
    delta = jnp.sum(probs_b.astype(jnp.float32) * dprobs, axis=-1, keepdims=True)
    dscores = (probs * (dprobs - delta) * scale).astype(jnp.bfloat16)
    dq = dot(dscores, k, NN)
    dk = dot(dscores, q, TN)
    dv = dot(probs_b, g, TN)
    return dq, dk, dv


def kernel(sections, ranks, ckpt, grad, out, qkv, gbuf, obuf, msend, mrecv, gsend, grecv, osend, orecv):
    p = lax.axis_index("pipe")
    t = lax.axis_index("tp")
    mirror = sections - 1 - p
    rows = ckpt.shape[1]
    owned = ckpt.shape[2] // ranks
    chunks = qkv.shape[0]
    width = qkv.shape[3]
    mine = pl.ds(pl.multiple_of(t * rows, rows), rows)

    def peer(k):
        return lax.rem(t + k, ranks)

    def features(rank, c):
        return pl.ds(pl.multiple_of(rank * owned + c * width, width), width)

    barrier = pltpu.get_barrier_semaphore()
    for k in range(ranks):
        pl.semaphore_signal(barrier, inc=1, device_id=(mirror, peer(k)), device_id_type=MESH)
    for k in range(1, ranks):
        pl.semaphore_signal(barrier, inc=1, device_id=(p, peer(k)), device_id_type=MESH)
    pl.semaphore_wait(barrier, 2 * ranks - 1)

    def fetch(c):
        pltpu.make_async_copy(grad.at[:, features(t, c)], gbuf.at[c, mine, :], grecv.at[c]).start()
        for k in range(ranks):
            pltpu.make_async_remote_copy(
                src_ref=ckpt.at[:, :, features(peer(k), c)],
                dst_ref=qkv.at[c, :, mine, :],
                send_sem=msend,
                recv_sem=mrecv.at[c],
                device_id=(mirror, peer(k)),
                device_id_type=MESH,
            ).start()
        for k in range(1, ranks):
            pltpu.make_async_remote_copy(
                src_ref=grad.at[:, features(peer(k), c)],
                dst_ref=gbuf.at[c, mine, :],
                send_sem=gsend,
                recv_sem=grecv.at[c],
                device_id=(p, peer(k)),
                device_id_type=MESH,
            ).start()

    def arrived(ref, sem):
        pltpu.make_async_copy(ref, ref, sem).wait()

    for c in range(AHEAD):
        fetch(c)

    @pl.loop(0, chunks)
    def _(c):
        arrived(qkv.at[c], mrecv.at[c])
        arrived(gbuf.at[c], grecv.at[c])

        @pl.when(c + AHEAD < chunks)
        def _():
            fetch(c + AHEAD)

        for h in range(width // HEAD_DIM):
            lanes = slice(h * HEAD_DIM, (h + 1) * HEAD_DIM)
            dq, dk, dv = head_back(qkv[c, 0, :, lanes], qkv[c, 1, :, lanes], qkv[c, 2, :, lanes], gbuf[c, :, lanes])
            obuf[c, 0, :, lanes] = dq.astype(jnp.bfloat16)
            obuf[c, 1, :, lanes] = dk.astype(jnp.bfloat16)
            obuf[c, 2, :, lanes] = dv.astype(jnp.bfloat16)

        for k in range(1, ranks):
            theirs = pl.ds(pl.multiple_of(peer(k) * rows, rows), rows)
            pltpu.make_async_remote_copy(
                src_ref=obuf.at[c, :, theirs, :],
                dst_ref=out.at[:, :, features(t, c)],
                send_sem=osend,
                recv_sem=orecv,
                device_id=(p, peer(k)),
                device_id_type=MESH,
            ).start()
        pltpu.make_async_copy(obuf.at[c, :, mine, :], out.at[:, :, features(t, c)], orecv).start()

    arrived(ckpt, msend)
    most = pl.ds(0, (ranks - 1) * owned)
    arrived(grad.at[:, most], gsend)
    arrived(out.at[:, :, most], osend)
    arrived(out, orecv)


def on_device(ckpt, grad, width=HEAD_DIM):
    sections = lax.axis_size("pipe")
    ranks = lax.axis_size("tp")
    _, parts, rows, features = ckpt.shape
    length = rows * ranks
    owned = features // ranks
    chunks = owned // width
    out = pl.pallas_call(
        functools.partial(kernel, sections, ranks),
        out_shape=jax.ShapeDtypeStruct((parts, rows, features), jnp.bfloat16),
        in_specs=[pl.BlockSpec(memory_space=pl.ANY)] * 2,
        out_specs=pl.BlockSpec(memory_space=pl.ANY),
        scratch_shapes=[
            pltpu.VMEM((chunks, parts, length, width), jnp.bfloat16),
            pltpu.VMEM((chunks, length, width), jnp.bfloat16),
            pltpu.VMEM((chunks, parts, length, width), jnp.bfloat16),
            pltpu.SemaphoreType.DMA,
            pltpu.SemaphoreType.DMA((chunks,)),
            pltpu.SemaphoreType.DMA,
            pltpu.SemaphoreType.DMA((chunks,)),
            pltpu.SemaphoreType.DMA,
            pltpu.SemaphoreType.DMA,
        ],
        compiler_params=pltpu.CompilerParams(
            collective_id=0, has_side_effects=True, vmem_limit_bytes=56 * 2**20
        ),
    )(ckpt[0], grad[0])
    return out[None]


def solution(mesh):
    in_specs = (P("pipe", None, "tp", None), P("pipe", "tp", None))
    out_specs = P("pipe", None, "tp", None)
    return jax.shard_map(
        on_device, mesh=mesh, in_specs=in_specs, out_specs=out_specs, check_vma=False
    )
```

profile of v0, /device:TPU:1, one launch (start us, length us, event | category | flops | bytes accessed | tf_op | source)
XLA Modules:
  0.0 262.1 jit_solution(4569388937984546615)
XLA Ops:
  0.0 257.1 %shard_map.28 = bf16[3,128,6144]{2,1,0:T(8,128)(2,1)} custom-call(bf16[3,128,6144]{2,1,0:T(8,128)(2,1)} %bitcast.4, bf16[128,6144]{1,0:T(8,128)(2,1)} %bitcast.5), custom_call_target="tpu_custom_call" | custom-call | tf_op jit(solution)/shard_map/pallas_call | solution.py:134
  257.1 5.1 %copy.4 = bf16[1,3,128,6144]{3,2,1,0:T(8,128)(2,1)} copy(bf16[1,3,128,6144]{3,2,1,0:T(8,128)(2,1)} %bitcast.3) | data formatting | bytes 9437184
where the time goes:
time: 262 us
  Pallas kernels  257 us (98%)
  local copies, waits for them, and re-layouts  5.05 us (2%)
    pallas_call x1, Pallas kernels, on_device(): pl.pallas_call(functools.partial(kernel, sections, ranks), out_shape=jax....  257 us

commit v1 on v0

--- a/solution.py
+++ b/solution.py
@@ -9,7 +9,8 @@
 
 HEAD_DIM = 128
 MESH = pl.DeviceIdType.MESH
-AHEAD = 3
+EARLY = 3
+LIMIT = 59
 NT = (((1,), (1,)), ((), ()))
 NN = (((1,), (0,)), ((), ()))
 TN = (((0,), (0,)), ((), ()))
@@ -39,7 +40,7 @@
     return dq, dk, dv
 
 
-def kernel(sections, ranks, ckpt, grad, out, qkv, gbuf, obuf, msend, mrecv, gsend, grecv, osend, orecv):
+def kernel(sections, ranks, ckpt, grad, out, qkv, gbuf, obuf, msend, mrecv, gsend, grecv, osend, orecv, ready):
     p = lax.axis_index("pipe")
     t = lax.axis_index("tp")
     mirror = sections - 1 - p
@@ -55,24 +56,8 @@
     def features(rank, c):
         return pl.ds(pl.multiple_of(rank * owned + c * width, width), width)
 
-    barrier = pltpu.get_barrier_semaphore()
-    for k in range(ranks):
-        pl.semaphore_signal(barrier, inc=1, device_id=(mirror, peer(k)), device_id_type=MESH)
-    for k in range(1, ranks):
-        pl.semaphore_signal(barrier, inc=1, device_id=(p, peer(k)), device_id_type=MESH)
-    pl.semaphore_wait(barrier, 2 * ranks - 1)
-
-    def fetch(c):
+    def fetch_grad(c):
         pltpu.make_async_copy(grad.at[:, features(t, c)], gbuf.at[c, mine, :], grecv.at[c]).start()
-        for k in range(ranks):
-            pltpu.make_async_remote_copy(
-                src_ref=ckpt.at[:, :, features(peer(k), c)],
-                dst_ref=qkv.at[c, :, mine, :],
-                send_sem=msend,
-                recv_sem=mrecv.at[c],
-                device_id=(mirror, peer(k)),
-                device_id_type=MESH,
-            ).start()
         for k in range(1, ranks):
             pltpu.make_async_remote_copy(
                 src_ref=grad.at[:, features(peer(k), c)],
@@ -83,20 +68,56 @@
                 device_id_type=MESH,
             ).start()
 
+    def fetch_mirror(c):
+        for k in range(ranks):
+            pltpu.make_async_remote_copy(
+                src_ref=ckpt.at[:, :, features(peer(k), c)],
+                dst_ref=qkv.at[c, :, mine, :],
+                send_sem=msend,
+                recv_sem=mrecv.at[c],
+                device_id=(mirror, peer(k)),
+                device_id_type=MESH,
+            ).start()
+
+    upper = lax.rem(lax.div(p, 2), 2)
+    barrier = pltpu.get_barrier_semaphore()
+    for k in range(1, ranks):
+        pl.semaphore_signal(barrier, inc=1, device_id=(p, peer(k)), device_id_type=MESH)
+
+    @pl.when(upper == 0)
+    def _():
+        for k in range(ranks):
+            pl.semaphore_signal(barrier, inc=1, device_id=(mirror, peer(k)), device_id_type=MESH)
+        pl.semaphore_wait(barrier, ranks - 1)
+
+    @pl.when(upper == 1)
+    def _():
+        pl.semaphore_wait(barrier, 2 * ranks - 1)
+        for k in range(ranks):
+            pl.semaphore_signal(ready, inc=1, device_id=(mirror, peer(k)), device_id_type=MESH)
+
+    for c in range(EARLY):
+        fetch_grad(c)
+
+    @pl.when(upper == 0)
+    def _():
+        pl.semaphore_wait(ready, ranks)
+
+    @pl.loop(0, chunks)
+    def _(c):
+        fetch_mirror(c)
+
+        @pl.when(c + EARLY < chunks)
+        def _():
+            fetch_grad(c + EARLY)
+
     def arrived(ref, sem):
         pltpu.make_async_copy(ref, ref, sem).wait()
-
-    for c in range(AHEAD):
-        fetch(c)
 
     @pl.loop(0, chunks)
     def _(c):
         arrived(qkv.at[c], mrecv.at[c])
         arrived(gbuf.at[c], grecv.at[c])
-
-        @pl.when(c + AHEAD < chunks)
-        def _():
-            fetch(c + AHEAD)
 
         for h in range(width // HEAD_DIM):
             lanes = slice(h * HEAD_DIM, (h + 1) * HEAD_DIM)
@@ -133,9 +154,9 @@
     chunks = owned // width
     out = pl.pallas_call(
         functools.partial(kernel, sections, ranks),
-        out_shape=jax.ShapeDtypeStruct((parts, rows, features), jnp.bfloat16),
+        out_shape=pltpu.VMEM((parts, rows, features), jnp.bfloat16),
         in_specs=[pl.BlockSpec(memory_space=pl.ANY)] * 2,
-        out_specs=pl.BlockSpec(memory_space=pl.ANY),
+        out_specs=pl.BlockSpec(memory_space=pltpu.VMEM),
         scratch_shapes=[
             pltpu.VMEM((chunks, parts, length, width), jnp.bfloat16),
             pltpu.VMEM((chunks, length, width), jnp.bfloat16),
@@ -146,9 +167,10 @@
             pltpu.SemaphoreType.DMA((chunks,)),
             pltpu.SemaphoreType.DMA,
             pltpu.SemaphoreType.DMA,
+            pltpu.SemaphoreType.REGULAR,
         ],
         compiler_params=pltpu.CompilerParams(
-            collective_id=0, has_side_effects=True, vmem_limit_bytes=56 * 2**20
+            collective_id=0, has_side_effects=True, vmem_limit_bytes=LIMIT * 2**20
         ),
     )(ckpt[0], grad[0])
     return out[None]

time: 262 us -> 249 us (0.950); the launches traced: 262 us -> 244 us
  Pallas kernels: 257 us -> 242 us
  local copies, waits for them, and re-layouts: 5.05 us -> 2.19 us
    pallas_call x1, Pallas kernels: 257 us -> 242 us  [on_device(): pl.pallas_call(functools.partial(kernel, sections, ranks), out_shape=pltp...]
    unnamed x1, local copies, waits for them, and re-layouts: 5.05 us -> 2.19 us
where the time goes in v1:
time: 249 us; the launch traced here: 244 us
  Pallas kernels  242 us (97%)
    pallas_call x1, Pallas kernels, on_device(): pl.pallas_call(functools.partial(kernel, sections, ranks), out_shape=pltp...  242 us

profile of v1, /device:TPU:1, one launch (start us, length us, event | category | flops | bytes accessed | tf_op | source)
XLA Modules:
  0.0 244.3 jit_solution(12320924416951761496)
XLA Ops:
  0.0 242.1 %shard_map.28 = bf16[3,128,6144]{2,1,0:T(8,128)(2,1)S(1)} custom-call(bf16[3,128,6144]{2,1,0:T(8,128)(2,1)} %bitcast.4, bf16[128,6144]{1,0:T(8,128)(2,1)} %bitcast.5), custom_call_target="tpu_custom_call" | custom-call | tf_op jit(solution)/shard_map/pallas_call | solution.py:155
  242.1 2.2 copy.4

commit v2 on v1

--- a/solution.py
+++ b/solution.py
@@ -10,7 +10,7 @@
 HEAD_DIM = 128
 MESH = pl.DeviceIdType.MESH
 EARLY = 3
-LIMIT = 59
+PACE = 3
 NT = (((1,), (1,)), ((), ()))
 NN = (((1,), (0,)), ((), ()))
 TN = (((0,), (0,)), ((), ()))
@@ -79,18 +79,20 @@
                 device_id_type=MESH,
             ).start()
 
-    upper = lax.rem(lax.div(p, 2), 2)
+    place = lax.div(p, 16) + lax.rem(lax.div(p, 4), 4)
+    half = lax.rem(lax.div(p, 2), 2)
+    answers = 2 * place + 7 * half >= 10
     barrier = pltpu.get_barrier_semaphore()
     for k in range(1, ranks):
         pl.semaphore_signal(barrier, inc=1, device_id=(p, peer(k)), device_id_type=MESH)
 
-    @pl.when(upper == 0)
+    @pl.when(jnp.logical_not(answers))
     def _():
         for k in range(ranks):
             pl.semaphore_signal(barrier, inc=1, device_id=(mirror, peer(k)), device_id_type=MESH)
         pl.semaphore_wait(barrier, ranks - 1)
 
-    @pl.when(upper == 1)
+    @pl.when(answers)
     def _():
         pl.semaphore_wait(barrier, 2 * ranks - 1)
         for k in range(ranks):
@@ -99,7 +101,7 @@
     for c in range(EARLY):
         fetch_grad(c)
 
-    @pl.when(upper == 0)
+    @pl.when(jnp.logical_not(answers))
     def _():
         pl.semaphore_wait(ready, ranks)
 
@@ -107,9 +109,10 @@
     def _(c):
         fetch_mirror(c)
 
-        @pl.when(c + EARLY < chunks)
-        def _():
-            fetch_grad(c + EARLY)
+        for j in range(PACE):
+            @pl.when(EARLY + c * PACE + j < chunks)
+            def _():
+                fetch_grad(EARLY + c * PACE + j)
 
     def arrived(ref, sem):
         pltpu.make_async_copy(ref, ref, sem).wait()
@@ -170,7 +173,7 @@
             pltpu.SemaphoreType.REGULAR,
         ],
         compiler_params=pltpu.CompilerParams(
-            collective_id=0, has_side_effects=True, vmem_limit_bytes=LIMIT * 2**20
+            collective_id=0, has_side_effects=True, vmem_limit_bytes=59 * 2**20
         ),
     )(ckpt[0], grad[0])
     return out[None]

time: 249 us -> 247 us (level)
  no operation moved by 1% of the time
where the time goes in v2:
time: 247 us; the launch traced here: 245 us
  Pallas kernels  243 us (98%)
    pallas_call x1, Pallas kernels, on_device(): pl.pallas_call(functools.partial(kernel, sections, ranks), out_shape=pltp...  243 us

profile of v2, /device:TPU:1, one launch (start us, length us, event | category | flops | bytes accessed | tf_op | source)
XLA Modules:
  0.0 244.7 jit_solution(6882422881468859541)
XLA Ops:
  0.0 242.5 %shard_map.28 = bf16[3,128,6144]{2,1,0:T(8,128)(2,1)S(1)} custom-call(bf16[3,128,6144]{2,1,0:T(8,128)(2,1)} %bitcast.4, bf16[128,6144]{1,0:T(8,128)(2,1)} %bitcast.5), custom_call_target="tpu_custom_call" | custom-call | tf_op jit(solution)/shard_map/pallas_call | solution.py:158
  242.6 2.2 copy.4

commit v3 on v2

--- a/solution.py
+++ b/solution.py
@@ -81,7 +81,7 @@
 
     place = lax.div(p, 16) + lax.rem(lax.div(p, 4), 4)
     half = lax.rem(lax.div(p, 2), 2)
-    answers = 2 * place + 7 * half >= 10
+    answers = 2 * place + 9 * half >= 11
     barrier = pltpu.get_barrier_semaphore()
     for k in range(1, ranks):
         pl.semaphore_signal(barrier, inc=1, device_id=(p, peer(k)), device_id_type=MESH)

time: 247 us -> 247 us (level)
  no operation moved by 1% of the time
where the time goes in v3:
time: 247 us; the launch traced here: 245 us
  Pallas kernels  243 us (98%)
    pallas_call x1, Pallas kernels, on_device(): pl.pallas_call(functools.partial(kernel, sections, ranks), out_shape=pltp...  243 us

profile of v3, /device:TPU:1, one launch (start us, length us, event | category | flops | bytes accessed | tf_op | source)
XLA Modules:
  0.0 244.7 jit_solution(13584826701964431267)
XLA Ops:
  0.0 242.5 %shard_map.28 = bf16[3,128,6144]{2,1,0:T(8,128)(2,1)S(1)} custom-call(bf16[3,128,6144]{2,1,0:T(8,128)(2,1)} %bitcast.4, bf16[128,6144]{1,0:T(8,128)(2,1)} %bitcast.5), custom_call_target="tpu_custom_call" | custom-call | tf_op jit(solution)/shard_map/pallas_call | solution.py:158
  242.6 2.2 copy.4

commit v4 on v3

--- a/solution.py
+++ b/solution.py
@@ -9,7 +9,8 @@
 
 HEAD_DIM = 128
 MESH = pl.DeviceIdType.MESH
-EARLY = 3
+GREETER = 4
+ANSWERER = 2
 PACE = 3
 NT = (((1,), (1,)), ((), ()))
 NN = (((1,), (0,)), ((), ()))
@@ -98,7 +99,10 @@
         for k in range(ranks):
             pl.semaphore_signal(ready, inc=1, device_id=(mirror, peer(k)), device_id_type=MESH)
 
-    for c in range(EARLY):
+    early = lax.select(answers, ANSWERER, GREETER)
+
+    @pl.loop(0, early)
+    def _(c):
         fetch_grad(c)
 
     @pl.when(jnp.logical_not(answers))
@@ -110,9 +114,9 @@
         fetch_mirror(c)
 
         for j in range(PACE):
-            @pl.when(EARLY + c * PACE + j < chunks)
+            @pl.when(early + c * PACE + j < chunks)
             def _():
-                fetch_grad(EARLY + c * PACE + j)
+                fetch_grad(early + c * PACE + j)
 
     def arrived(ref, sem):
         pltpu.make_async_copy(ref, ref, sem).wait()

time: 247 us -> 247 us (level)
  no operation moved by 1% of the time
where the time goes in v4:
time: 247 us; the launch traced here: 244 us
  Pallas kernels  242 us (98%)
    pallas_call x1, Pallas kernels, on_device(): pl.pallas_call(functools.partial(kernel, sections, ranks), out_shape=pltp...  242 us

profile of v4, /device:TPU:1, one launch (start us, length us, event | category | flops | bytes accessed | tf_op | source)
XLA Modules:
  0.0 244.3 jit_solution(10794029676595799810)
XLA Ops:
  0.0 242.2 %shard_map.28 = bf16[3,128,6144]{2,1,0:T(8,128)(2,1)S(1)} custom-call(bf16[3,128,6144]{2,1,0:T(8,128)(2,1)} %bitcast.4, bf16[128,6144]{1,0:T(8,128)(2,1)} %bitcast.5), custom_call_target="tpu_custom_call" | custom-call | tf_op jit(solution)/shard_map/pallas_call | solution.py:162
  242.2 2.2 copy.4
